TPU v7x, 32 devices: a whole 2x2x4 slice. The times are simulated.
32 devices in a mesh: dp: 4 (over y, x), expert: 8 (over z, core).
Axes of the slice: x: 2, y: 2, z: 4, core: 2. Of those that a mesh axis runs over, the one named last changes fastest.
Arguments:
- tokens: bfloat16 [4096, 3584], P(('dp', 'expert')), may hold values from -6 to 6
- cotangent: bfloat16 [4096, 3584], P(('dp', 'expert')), may hold values from -0.375 to 0.375
- gate_scale: float32 [4096], P(('dp', 'expert')), may hold values from 0.2 to 1
- expert_index: int32 [4096], P(('dp', 'expert')), may hold values from 0 to 7, as said below
- hot_index: int32 [8], replicated, may hold values from 0 to 7, as said below
- w_gate: bfloat16 [8, 3584, 1024], P('expert', None, 'dp'), may hold values from -0.09375 to 0.09375
- w_up: bfloat16 [8, 3584, 1024], P('expert', None, 'dp'), may hold values from -0.09375 to 0.09375
- w_down: bfloat16 [8, 1024, 3584], P('expert', 'dp'), may hold values from -0.1875 to 0.1875
Outputs:
- grad_gate: bfloat16 [8, 3584, 1024], P('expert', None, 'dp')
- grad_up: bfloat16 [8, 3584, 1024], P('expert', None, 'dp')
- grad_down: bfloat16 [8, 1024, 3584], P('expert', 'dp')
- hot_grads: bfloat16 [1, 3584, 3, 1024], P(None, 'expert', None, 'dp')
Inputs may be any that keep to these rules, and one draw needn't show every extreme that they name: `expert_index`: among the 128 tokens of one device (aligned blocks of rows), at most 24 are routed to any one expert other than hot_index[0], and from 24 to 48 to hot_index[0]. In every draw each group of devices sharing a dp index has an expert that receives exactly 24 tokens from each of its devices, and some devices route exactly 48 tokens to hot_index[0]. `hot_index`: A permutation of the 8 experts; its first entry is the replicated expert, to which every device routes at least as many tokens as to any other expert.
All inputs are finite; a program needn't handle non-finite values.
Results may differ from a plain program's by a relative error of at most 0.0058.
Values may be sent and summed in bfloat16 or wider, within the bound.
No kernel may reach another device: no remote copies, remote signals or barrier semaphores. Data moves between devices by JAX's collectives and lax.ppermute only.
A program may use at most 128 MiB of HBM per device.

v0:
```python
import functools

import jax
import jax.numpy as jnp
from jax import lax
from jax.experimental import pallas as pl
from jax.experimental.pallas import tpu as pltpu
from jax.sharding import PartitionSpec as P

CONTRACT_ROWS = (((0,), (0,)), ((), ()))


def spread(block, axis, source):
    block = jnp.where(lax.axis_index(axis) == source, block, jnp.zeros_like(block))
    return lax.psum(block, axis)


def expert_terms(row_tokens, row_grads, gate_matrix, up_matrix, down_matrix):
    pre_gate = jnp.dot(row_tokens, gate_matrix, preferred_element_type=jnp.float32)
    pre_up = jnp.dot(row_tokens, up_matrix, preferred_element_type=jnp.float32)
    hidden_back = lax.dot_general(
        row_grads, down_matrix, (((1,), (1,)), ((), ())), preferred_element_type=jnp.float32
    )
    sigmoid_gate = jax.nn.sigmoid(pre_gate)
    activated = pre_gate * sigmoid_gate
    hidden = (activated * pre_up).astype(jnp.bfloat16)
    gate_grad = (
        hidden_back * pre_up * sigmoid_gate * (1.0 + pre_gate * (1.0 - sigmoid_gate))
    ).astype(jnp.bfloat16)
    up_grad = (hidden_back * activated).astype(jnp.bfloat16)
    return (hidden, gate_grad, up_grad)


def column_sum(left, right):
    return lax.dot_general(left, right, CONTRACT_ROWS, preferred_element_type=jnp.float32)


def route_rows(selector, values):
    return jnp.dot(selector, values, preferred_element_type=jnp.float32).astype(jnp.bfloat16)


def on_large_mesh(tokens, cotangent, gate_scale, expert_index, hot_index, w_gate, w_up, w_down):
    tok_rows, feature_width = tokens.shape
    experts = lax.axis_size("expert")
    capacity = 3 * tok_rows // (2 * experts)
    hot_capacity = 2 * capacity
    hot_expert = hot_index[0]
    route_grad = (gate_scale[:, None] * cotangent.astype(jnp.float32)).astype(jnp.bfloat16)
    is_hot = expert_index == hot_expert
    not_hot = jnp.logical_not(is_hot)
    owners = lax.broadcasted_iota(jnp.int32, (tok_rows, experts), 1)
    member = ((expert_index[:, None] == owners) & not_hot[:, None]).astype(jnp.int32)
    bucket_place = jnp.sum((jnp.cumsum(member, axis=0) - 1) * member, axis=1)
    slot_index = expert_index * capacity + bucket_place
    slot_grid = lax.broadcasted_iota(jnp.int32, (experts * capacity, tok_rows), 0)
    cold_map = ((slot_grid == slot_index[None, :]) & not_hot[None, :]).astype(jnp.bfloat16)
    hot_place = jnp.cumsum(is_hot.astype(jnp.int32)) - 1
    hot_grid = lax.broadcasted_iota(jnp.int32, (hot_capacity, tok_rows), 0)
    hot_map = ((hot_grid == hot_place[None, :]) & is_hot[None, :]).astype(jnp.bfloat16)
    send_tokens = route_rows(cold_map, tokens).reshape(experts, capacity, feature_width)
    send_grads = route_rows(cold_map, route_grad).reshape(experts, capacity, feature_width)
    own_hot_tokens = route_rows(hot_map, tokens)
    own_hot_grads = route_rows(hot_map, route_grad)
    arrived_tokens, arrived_grads = (
        lax.all_to_all(send_tokens, "expert", split_axis=0, concat_axis=0, tiled=True),
        lax.all_to_all(send_grads, "expert", split_axis=0, concat_axis=0, tiled=True),
    )
    cold_tokens, cold_grads, hot_tokens, hot_row_grads = (
        lax.all_gather(
            arrived_tokens.reshape(experts * capacity, feature_width), "dp", axis=0, tiled=True
        ),
        lax.all_gather(
            arrived_grads.reshape(experts * capacity, feature_width), "dp", axis=0, tiled=True
        ),
        lax.all_gather(own_hot_tokens, "dp", axis=0, tiled=True),
        lax.all_gather(own_hot_grads, "dp", axis=0, tiled=True),
    )
    shadow_gate, shadow_up, shadow_down = (
        spread(w_gate[0], "expert", hot_expert),
        spread(w_up[0], "expert", hot_expert),
        spread(w_down[0], "expert", hot_expert),
    )
    hidden, gate_grad, up_grad = expert_terms(
        cold_tokens, cold_grads, w_gate[0], w_up[0], w_down[0]
    )
    grad_gate = column_sum(cold_tokens, gate_grad).astype(jnp.bfloat16)
    grad_up = column_sum(cold_tokens, up_grad).astype(jnp.bfloat16)
    grad_down = column_sum(hidden, cold_grads).astype(jnp.bfloat16)
    hot_hidden, hot_gate_grad, hot_up_grad = expert_terms(
        hot_tokens, hot_row_grads, shadow_gate, shadow_up, shadow_down
    )
    gate_part = column_sum(hot_tokens, hot_gate_grad)
    up_part = column_sum(hot_tokens, hot_up_grad)
    down_part = column_sum(hot_row_grads, hot_hidden)
    owned_part = lax.psum_scatter(
        jnp.stack([gate_part, up_part, down_part], axis=1),
        "expert",
        scatter_dimension=0,
        tiled=True,
    )
    hot_grads = owned_part.astype(jnp.bfloat16)[None]
    return (grad_gate[None], grad_up[None], grad_down[None], hot_grads)


ANYWHERE = pl.BlockSpec(memory_space=pltpu.HBM)
VMEM_LIMIT = 56 * 2**20


def together(passed, awaited=()):
    n = len(passed)
    return pl.pallas_call(
        lambda *refs: None,
        out_shape=[jax.ShapeDtypeStruct(a.shape, a.dtype) for a in passed],
        in_specs=[pl.BlockSpec(memory_space=pl.ANY)] * (n + len(awaited)),
        out_specs=[pl.BlockSpec(memory_space=pl.ANY)] * n,
        input_output_aliases={i: i for i in range(n)},
        name="together",
    )(*passed, *awaited)


def divisor(size, most, unit):
    return max(d for d in range(unit, most + 1, unit) if size % d == 0)


def terms_kernel(kind, plan, n_sources, block_rows, block_columns, *refs):
    flags, refs = refs[0], refs[1:]
    sources, refs = refs[:n_sources], refs[n_sources:]
    sets = 2 if kind == "hot" else 1
    weight_refs, refs = refs[: 3 * sets], refs[3 * sets :]
    in_sem, w_sem, out_sem = refs[-3:]
    refs = refs[:-3]
    if kind == "cold":
        *outs, done, tok, grd, gate_w, up_w, down_w, gate_up_t, hidden_t, res_a, res_b, res_c = refs
    else:
        *outs, tok, grd, gate_w, up_w, down_w, gate_up_t, hidden_t, res_a, res_b, res_c = refs
    rows, width = tok.shape
    hidden_width = gate_w.shape[1]
    core = flags[0]
    column_blocks = width // block_columns

    def copies(choice, core_value, first_piece, last_piece):
        at, result = 0, []
        for k, (by_core, count) in enumerate(plan[choice]):
            if first_piece <= k < last_piece:
                for which, buffer in enumerate((tok, grd)):
                    source, first = by_core[core_value][which]
                    result.append(
                        pltpu.make_async_copy(
                            sources[source].at[pl.ds(first, count)],
                            buffer.at[pl.ds(at, count)],
                            in_sem.at[2 * k + which],
                        )
                    )
            at += count
        return result

    def span_of(i):
        return pl.ds(i * block_columns, block_columns)

    def work():
        def fetched(which):
            return [
                pltpu.make_async_copy(weight_refs[3 * which + i], buffer, w_sem.at[i])
                for i, buffer in enumerate((gate_w, up_w, down_w))
            ]

        weights = fetched(0)
        for which in range(sets):

            @pl.when(flags[3] == which)
            def _():
                for copy in fetched(which):
                    copy.start()

        sizes = [entry[-1] for entry in plan[0]]

        def fetch(first_piece, last_piece):
            for choice in range(len(plan)):
                for core_value in range(2):

                    @pl.when((flags[2] == choice) & (core == core_value))
                    def _():
                        for copy in copies(choice, core_value, first_piece, last_piece):
                            copy.start()

        def needed(block):
            return next(
                k for k in range(len(sizes) + 1) if sum(sizes[:k]) >= (block + 1) * block_rows
            )

        fetch(0, needed(0))
        for copy in weights:
            copy.wait()

        def forward(first_row):
            span = pl.ds(first_row, block_rows)
            row_tokens, row_grads = tok[span, :], grd[span, :]
            pre_gate = jnp.dot(row_tokens, gate_w[...], preferred_element_type=jnp.float32)
            pre_up = jnp.dot(row_tokens, up_w[...], preferred_element_type=jnp.float32)
            hidden_back = lax.dot_general(
                row_grads, down_w[...], (((1,), (1,)), ((), ())), preferred_element_type=jnp.float32
            )
            sigmoid_gate = jax.nn.sigmoid(pre_gate)
            activated = pre_gate * sigmoid_gate
            hidden = activated * pre_up
            gate_grad = hidden_back * pre_up * sigmoid_gate * (1.0 + pre_gate * (1.0 - sigmoid_gate))
            up_grad = hidden_back * activated
            hidden_t[:, span] = hidden.T.astype(jnp.bfloat16)
            gate_up_t[pl.ds(0, hidden_width), span] = gate_grad.T.astype(jnp.bfloat16)
            gate_up_t[pl.ds(hidden_width, hidden_width), span] = up_grad.T.astype(jnp.bfloat16)

        if kind == "cold":
            fetch(needed(0), len(sizes))
            for copy in copies(0, 0, 0, len(sizes)):
                copy.wait()

            def each(i, carry):
                forward(pl.multiple_of(i * block_rows, block_rows))
                return carry

            lax.fori_loop(0, rows // block_rows, each, 0)
        else:
            arrived = 0
            for block in range(rows // block_rows):
                for copy in copies(0, 0, arrived, needed(block)):
                    copy.wait()
                arrived = needed(block)
                if block == 0:
                    fetch(arrived, len(sizes))
                forward(block * block_rows)

        def products(span):
            sums = jnp.dot(gate_up_t[...], tok[:, span], preferred_element_type=jnp.float32)
            downs = jnp.dot(hidden_t[...], grd[:, span], preferred_element_type=jnp.float32)
            return sums, downs

        if kind == "cold":

            def columns(i, carry):
                span = pl.ds(pl.multiple_of(i * block_columns, block_columns), block_columns)
                sums, downs = products(span)
                sums = sums.T.astype(jnp.bfloat16)
                res_a[span, :] = sums[:, :hidden_width]
                res_b[span, :] = sums[:, hidden_width:]
                res_c[:, span] = downs.astype(jnp.bfloat16)
                return carry

            lax.fori_loop(0, column_blocks, columns, 0)
            return
        chips = len(outs)
        part = width // (2 * chips)
        lead = part % 128
        window = part + lead
        for chip in range(chips):
            start = 2 * part * chip + core * (part - lead)
            span = pl.ds(pl.multiple_of(start, 128), window)
            here = pl.ds(chip * window, window)
            sums, downs = products(span)
            sums = sums.T.astype(jnp.bfloat16)
            res_a[here, :] = sums[:, :hidden_width]
            res_b[here, :] = sums[:, hidden_width:]
            res_c[here, :] = downs.T.astype(jnp.bfloat16)
        written = [
            pltpu.make_async_copy(
                res.at[pl.ds(pl.multiple_of(chip * window + core * lead, 16), part)],
                outs[chip].at[q],
                out_sem.at[3 * chip + q],
            )
            for chip in range(chips)
            for q, res in enumerate((res_a, res_b, res_c))
        ]
        for copy in written:
            copy.start()
        for copy in written:
            copy.wait()

    @pl.when(flags[1] == 1)
    def _():
        work()

    if kind == "cold":

        @pl.when(flags[1] == 0)
        def _():
            for res in (res_a, res_b, res_c):
                res[...] = jnp.zeros_like(res)

        written = [
            pltpu.make_async_copy(res, out, out_sem.at[i])
            for i, (res, out) in enumerate(zip((res_a, res_b, res_c), outs))
        ]
        for copy in written:
            copy.start()
        done[...] = jnp.zeros_like(done)
        for copy in written:
            copy.wait()


def expert_call(kind, flags, plan, blocks, sources, weights):
    width, hidden_width = weights[0].shape
    rows = sum(entry[-1] for entry in plan[0])
    block_rows = divisor(rows, 384 if kind == "hot" else 128, 128)
    block_columns = divisor(width, 512 if kind == "hot" else 256, 128)
    bf16 = jnp.bfloat16
    scratch = [
        pltpu.VMEM((rows, width), bf16),
        pltpu.VMEM((rows, width), bf16),
        pltpu.VMEM((width, hidden_width), bf16),
        pltpu.VMEM((width, hidden_width), bf16),
        pltpu.VMEM((hidden_width, width), bf16),
        pltpu.VMEM((2 * hidden_width, rows), bf16),
        pltpu.VMEM((hidden_width, rows), bf16),
    ]
    result = pltpu.VMEM((width, hidden_width), bf16)
    if kind == "hot":
        chips = blocks // 2
        part = width // blocks
        out_shape = [jax.ShapeDtypeStruct((3, part, hidden_width), bf16)] * chips
        result = pltpu.VMEM((chips * (part + part % 128), hidden_width), bf16)
        scratch += [result, result, result]
    else:
        out_shape = [jax.ShapeDtypeStruct(w.shape, bf16) for w in weights[:3]]
        out_shape += [jax.ShapeDtypeStruct((8, 128), jnp.int32)]
        scratch += [result, result, pltpu.VMEM((hidden_width, width), bf16)]
    scratch += [
        pltpu.SemaphoreType.DMA((2 * len(plan[0]),)),
        pltpu.SemaphoreType.DMA((3,)),
        pltpu.SemaphoreType.DMA((3 * blocks,)),
    ]
    out_specs = [ANYWHERE] * len(out_shape)
    if kind == "cold":
        out_specs[-1] = pl.BlockSpec(memory_space=pltpu.VMEM)
    kernel = functools.partial(terms_kernel, kind, plan, len(sources), block_rows, block_columns)
    return pl.pallas_call(
        kernel,
        out_shape=out_shape,
        in_specs=[pl.BlockSpec(memory_space=pltpu.SMEM)]
        + [ANYWHERE] * (len(sources) + len(weights)),
        out_specs=out_specs,
        scratch_shapes=scratch,
        compiler_params=pltpu.CompilerParams(vmem_limit_bytes=VMEM_LIMIT),
        cost_estimate=pl.CostEstimate(
            flops=12 * rows * width * hidden_width,
            bytes_accessed=4 * rows * width + 12 * width * hidden_width,
            transcendentals=rows * hidden_width,
        ),
        name=kind + "_terms",
    )(flags, *sources, *weights)


def on_device(tokens, cotangent, gate_scale, expert_index, hot_index, w_gate, w_up, w_down):
    tok_rows, width = tokens.shape
    experts = lax.axis_size("expert")
    dp = lax.axis_size("dp")
    chips = experts // 2
    capacity = 3 * tok_rows // (2 * experts)
    if chips != 4 or dp != 4 or capacity % 8 != 0:
        return on_large_mesh(
            tokens, cotangent, gate_scale, expert_index, hot_index, w_gate, w_up, w_down
        )
    hot_expert = hot_index[0]
    me = lax.axis_index("expert")
    core, chip = me % 2, me // 2
    flat = [(i, j) for i in range(dp) for j in range(experts)]

    def place_of(i, j):
        return i * experts + j

    def swap(array):
        return lax.ppermute(array, "expert", [(j, j ^ 1) for j in range(experts)])

    def along(array, step):
        return lax.ppermute(array, "expert", [(j, j ^ (2 * step)) for j in range(experts)])

    def first_way(array):
        pairs = [(place_of(i, j), place_of(i ^ (2 if j % 2 else 1), j)) for i, j in flat]
        return lax.ppermute(array, ("dp", "expert"), pairs)

    def second_way(array):
        pairs = [(place_of(i, j), place_of(i ^ (1 if j % 2 else 2), j)) for i, j in flat]
        return lax.ppermute(array, ("dp", "expert"), pairs)

    route_grad = (gate_scale[:, None] * cotangent.astype(jnp.float32)).astype(jnp.bfloat16)
    own = jnp.where(core == 0, tokens, route_grad)
    other = jnp.where(core == 0, route_grad, tokens)
    sibling, sibling_index = swap(other), swap(expert_index)
    earlier = lax.broadcasted_iota(jnp.int32, (tok_rows, tok_rows), 1) < lax.broadcasted_iota(
        jnp.int32, (tok_rows, tok_rows), 0
    )

    def places(index):
        return jnp.sum(((index[:, None] == index[None, :]) & earlier).astype(jnp.int32), axis=1)

    index = jnp.concatenate([expert_index, sibling_index])
    place = jnp.concatenate([places(expert_index), places(sibling_index)])
    holder = jnp.concatenate([jnp.full((tok_rows,), core), jnp.full((tok_rows,), 1 - core)])
    values = jnp.concatenate([own, sibling], axis=0)
    message = 2 * capacity
    slots = lax.broadcasted_iota(jnp.int32, (message, 2 * tok_rows), 0)

    def selector(kind, step):
        target = chip ^ step
        expert = jnp.where(hot_expert // 2 == target, hot_expert, 2 * target)
        offset = 0
        if kind == "second":
            expert = expert ^ 1
        elif kind == "rest":
            expert, offset = hot_expert, capacity
        taken = (index == expert) & (place >= offset) & (place < offset + capacity)
        slot = place - offset + capacity * holder
        return ((slots == slot[None, :]) & taken[None, :]).astype(jnp.bfloat16)

    def rows(*wanted, of=values):
        return route_rows(jnp.concatenate([selector(*w) for w in wanted], axis=0), of)

    weights = (w_gate[0], w_up[0], w_down[0])
    is_owner = me == hot_expert
    owns = is_owner.astype(jnp.int32)
    zero = jnp.zeros((), jnp.int32)
    hot_chip = (hot_expert // 2 == chip).astype(jnp.int32)
    hot_flags = jnp.stack([core, hot_chip, zero, 1 - owns])
    sibling_weights = tuple(swap(w) for w in weights)

    unit_rows, hot_rows = 3 * message, 2 * message
    weights = (w_gate[0], w_up[0], w_down[0])
    is_owner = me == hot_expert
    owns = is_owner.astype(jnp.int32)
    zero = jnp.zeros((), jnp.int32)
    hot_chip = (hot_expert // 2 == chip).astype(jnp.int32)
    hot_flags = jnp.stack([core, hot_chip, zero, 1 - owns])
    sibling_weights = tuple(swap(w) for w in weights)

    lies = (
        (0, ((4, 0), (5, 0), (6, 0), (7, 0))),
        (8, ((12, 0), (13, 0), (14, 0), (22, 0))),
        (15, ((19, 0), (20, 0), (21, 0), (23, 0))),
        (24, ((28, 0), (29, 0), (30, 0), (31, 0))),
    )

    def pieces(unit, first, count):
        chosen = []
        for k, (array, at) in enumerate(lies[unit][1]):
            mine, theirs = (lies[unit][0] + k, first), (array, at + first)
            chosen.append((((mine, theirs), (theirs, mine)), count))
        return tuple(chosen)

    near_unit = rows(("first", 0), ("rest", 0))
    sent = {k: [rows((k, s)) for s in range(1, chips)] for k in ("first", "rest")}


    (near_unit,) = together([near_unit], sibling_weights)
    near_1, side_1 = first_way(near_unit), second_way(near_unit)
    got = [along(block, s) for s, block in enumerate(sent["first"], 1)]
    first_unit = jnp.concatenate(got, axis=0)
    near_unit, near_1, side_1, first_unit, *sent["rest"] = together(
        [near_unit, near_1, side_1, first_unit, *sent["rest"]]
    )
    far_1 = second_way(near_1)
    near_2, side_2 = first_way(first_unit), second_way(first_unit)
    got = [along(block, s) for s, block in enumerate(sent["rest"], 1)]
    (values,) = together([values], got[:1])
    own_second, *sent["second"] = [rows(("second", s), of=values) for s in range(chips)]
    swapped_1 = [swap(a) for a in (near_unit, side_1, near_1)]
    rest_unit = jnp.concatenate(got, axis=0)
    far_1, first_unit, near_2, side_2, rest_unit, *sent["second"] = together([
        far_1, first_unit, near_2, side_2, rest_unit, *sent["second"]
    ])
    far_2 = second_way(near_2)
    near_3, side_3 = first_way(rest_unit), second_way(rest_unit)
    got = [along(block, s) for s, block in enumerate(sent["second"], 1)]
    swapped_1.append(swap(far_1))
    swapped_2 = [swap(a) for a in (first_unit, side_2, near_2)]
    second_unit = jnp.concatenate([own_second] + got, axis=0)
    far_2, rest_unit, near_3, side_3, second_unit, *swapped_1 = together(
        [far_2, rest_unit, near_3, side_3, second_unit, *swapped_1]
    )
    far_3 = second_way(near_3)
    swapped_3 = [swap(a) for a in (rest_unit, side_3, near_3, far_2)]
    far_3, second_unit = together([far_3, second_unit])
    near_4, side_4 = first_way(second_unit), second_way(second_unit)
    far_3_swap = swap(far_3)

    sources = [near_unit, near_1, side_1, far_1, *swapped_1]
    sources += [first_unit, near_2, side_2, far_2, *swapped_2]
    sources += [rest_unit, near_3, side_3, far_3, *swapped_3, far_3_swap]
    kept = expert_call(
        "hot",
        hot_flags,
        (pieces(0, 0, hot_rows) + pieces(1, 0, unit_rows) + pieces(2, 0, unit_rows),),
        experts,
        sources,
        weights + sibling_weights,
    )
    second_swap = swap(second_unit)
    near_4, side_4, second_swap, *kept = together([near_4, side_4, second_swap, *kept])

    first_of_chip = jnp.where(hot_expert // 2 == chip, hot_expert % 2, 0)
    cold_flags = jnp.stack([core, 1 - owns, (first_of_chip != core).astype(jnp.int32), zero])
    first_plan = pieces(0, 0, message)
    for k in range(chips - 1):
        first_plan += pieces(1, k * message, message)
    second_plan = ()
    for k in range(chips):
        second_plan += pieces(3, k * message, message)

    def finish(owner, blocks, near_4, side_4, second_unit, second_swap, sources):
        others = sorted((z for z in range(chips) if z != owner), key=lambda z: -abs(z - owner))

        def send(z):
            pairs = [(2 * owner + c, 2 * z + c) for c in range(2)]
            return lax.ppermute(blocks[z], "expert", pairs)

        far_4 = second_way(near_4)
        near_swap, side_swap = swap(near_4), swap(side_4)
        got = [send(others[0])]
        (far_4,) = together([far_4], got)
        far_swap = swap(far_4)
        got += [send(z) for z in others[1:]]
        *cold, done = expert_call(
            "cold",
            cold_flags,
            (first_plan, second_plan),
            experts,
            sources
            + [second_unit, near_4, side_4, far_4, second_swap, side_swap, near_swap, far_swap],
            weights,
        )
        arrived = functools.reduce(jnp.add, got)
        return (*cold, jnp.where(chip == owner + done[0, 0], blocks[owner], arrived))

    grad_gate, grad_up, grad_down, hot_grads = lax.switch(
        hot_expert // 2,
        [functools.partial(finish, owner) for owner in range(chips)],
        kept,
        near_4,
        side_4,
        second_unit,
        second_swap,
        sources,
    )
    hot_grads = jnp.transpose(hot_grads, (1, 0, 2))
    return (grad_gate[None], grad_up[None], grad_down[None], hot_grads[None])


def solution(mesh):
    placed = (
        P(("dp", "expert"), None),
        P(("dp", "expert"), None),
        P(("dp", "expert")),
        P(("dp", "expert")),
        P(),
        P("expert", None, "dp"),
        P("expert", None, "dp"),
        P("expert", "dp", None),
    )
    return jax.shard_map(
        on_device,
        mesh=mesh,
        in_specs=placed,
        out_specs=(
            P("expert", None, "dp"),
            P("expert", None, "dp"),
            P("expert", "dp", None),
            P(None, "expert", None, "dp"),
        ),
        check_vma=False,
    )
```

profile of v0, /device:TPU:0, one launch (start us, length us, event | category | flops | bytes accessed | tf_op | source)
XLA Modules:
  0.0 232.3 jit_solution(14413031249427948760)
XLA Ops:
  1.2 3.0 %broadcast_select_fusion.1 = (bf16[128,3584]{1,0:T(8,128)(2,1)S(1)}, bf16[128,3584]{1,0:T(8,128)(2,1)}) fusion(bf16[128,3584]{1,0:T(8,128)(2,1)} %param.12, pred[]{:T(512)S(6)} %eq.233, bf16[128,3584]{1,0:T(8,128)(2,1)} %param.13, f32[128]{0:T(128)} %param.14), kind=kLoop, calls=%fused_computation.19 | loop fusion | flops 2293760 | bytes 3670529 | tf_op jit(solution)/shard_map/jit(_where)/select_n | solution.py:384
  7.6 2.3 %convolution_convert_fusion.8 = bf16[48,3584]{1,0:T(8,128)(2,1)} fusion(s32[256]{0:T(256)S(1)} %get-tuple-element.559, pred[256]{0:T(512)(128)(4,1)S(1)} %get-tuple-element.556, bf16[128,3584]{1,0:T(8,128)(2,1)} %collective-permute-done.29, bf16[128,3584]{1,0:T(8,128)(2,1)S(1)} %get-tuple-element.549), kind=kOutput, calls=%fused_computation.12 | convolution fusion | flops 91947008 | bytes 2180352 | tf_op jit(solution)/shard_map/dot_general | solution.py:39
  9.9 2.7 %collective-permute-start.35 = (bf16[48,3584]{1,0:T(8,128)(2,1)}, bf16[48,3584]{1,0:T(8,128)(2,1)}, u32[]{:S(2)}, u32[]{:S(2)}) collective-permute-start(bf16[48,3584]{1,0:T(8,128)(2,1)} %convolution_convert_fusion.8), channel_id=1, source_target_pairs={{0,2},{1,3},{2,0},{3,1},{4,6},{5,7},{6,4},{7,5},{8,10},{9,11},{10,... | collective-permute-start | bytes 1032200 | tf_op jit(solution)/shard_map/ppermute | solution.py:373
  12.6 2.3 %convolution_convert_fusion.7 = bf16[48,3584]{1,0:T(8,128)(2,1)} fusion(s32[256]{0:T(256)S(1)} %get-tuple-element.559, pred[256]{0:T(512)(128)(4,1)S(1)} %get-tuple-element.555, bf16[128,3584]{1,0:T(8,128)(2,1)} %collective-permute-done.29, bf16[128,3584]{1,0:T(8,128)(2,1)S(1)} %get-tuple-element.549), kind=kOutput, calls=%fused_computation.11 | convolution fusion | flops 91947008 | bytes 2180352 | tf_op jit(solution)/shard_map/dot_general | solution.py:39
  14.9 2.6 %collective-permute-start.36 = (bf16[48,3584]{1,0:T(8,128)(2,1)}, bf16[48,3584]{1,0:T(8,128)(2,1)}, u32[]{:S(2)}, u32[]{:S(2)}) collective-permute-start(bf16[48,3584]{1,0:T(8,128)(2,1)} %convolution_convert_fusion.7), channel_id=1, source_target_pairs={{0,4},{1,5},{2,6},{3,7},{4,0},{5,1},{6,2},{7,3},{8,12},{9,13},{10,... | collective-permute-start | bytes 1032200 | tf_op jit(solution)/shard_map/ppermute | solution.py:373
  17.5 2.3 %convolution_convert_fusion.6 = bf16[48,3584]{1,0:T(8,128)(2,1)} fusion(s32[256]{0:T(256)S(1)} %get-tuple-element.559, pred[256]{0:T(512)(128)(4,1)S(1)} %get-tuple-element.554, bf16[128,3584]{1,0:T(8,128)(2,1)} %collective-permute-done.29, bf16[128,3584]{1,0:T(8,128)(2,1)S(1)} %get-tuple-element.549), kind=kOutput, calls=%fused_computation.10 | convolution fusion | flops 91947008 | bytes 2180352 | tf_op jit(solution)/shard_map/dot_general | solution.py:39
  21.5 1.8 collective-permute-start.33
  27.9 13.9 %collective-permute-done.36 = bf16[48,3584]{1,0:T(8,128)(2,1)} collective-permute-done((bf16[48,3584]{1,0:T(8,128)(2,1)}, bf16[48,3584]{1,0:T(8,128)(2,1)}, u32[]{:S(2)}, u32[]{:S(2)}) %collective-permute-start.36) | collective-permute-done | bytes 344096 | tf_op jit(solution)/shard_map/ppermute | solution.py:373
  43.1 7.0 %collective-permute-start.41 = (bf16[48,3584]{1,0:T(8,128)(2,1)}, bf16[48,3584]{1,0:T(8,128)(2,1)S(1)}, u32[]{:S(2)}, u32[]{:S(2)}) collective-permute-start(bf16[48,3584]{1,0:T(8,128)(2,1)} %get-tuple-element.507), channel_id=1, source_target_pairs={{0,2},{1,3},{2,0},{3,1},{4,6},{5,7},{6,4},{7,5},{8,10},{9,11},{10,... | collective-permute-start | bytes 1032200 | tf_op jit(solution)/shard_map/ppermute | solution.py:373
  52.6 2.5 %pad_maximum_fusion.refs_0_ = bf16[256,3584]{1,0:T(8,128)(2,1)} fusion(bf16[128,3584]{1,0:T(8,128)(2,1)} %collective-permute-done.29, bf16[128,3584]{1,0:T(8,128)(2,1)S(1)} %copy-done.8), kind=kLoop, calls=%fused_computation.13 | loop fusion | flops 3670016 | bytes 3670016 | tf_op jit(solution)/shard_map/concatenate | solution.py:397
  58.1 6.0 %collective-permute-done.41.refs_1_ = bf16[48,3584]{1,0:T(8,128)(2,1)S(1)} collective-permute-done((bf16[48,3584]{1,0:T(8,128)(2,1)}, bf16[48,3584]{1,0:T(8,128)(2,1)S(1)}, u32[]{:S(2)}, u32[]{:S(2)}) %collective-permute-start.41) | collective-permute-done | bytes 344096 | tf_op jit(solution)/shard_map/ppermute | solution.py:373
  65.6 11.4 %collective-permute-done.42 = bf16[48,3584]{1,0:T(8,128)(2,1)S(1)} collective-permute-done((bf16[48,3584]{1,0:T(8,128)(2,1)}, bf16[48,3584]{1,0:T(8,128)(2,1)S(1)}, u32[]{:S(2)}, u32[]{:S(2)}) %collective-permute-start.42) | collective-permute-done | bytes 344096 | tf_op jit(solution)/shard_map/ppermute | solution.py:373
  78.6 2.8 %convolution_convert_fusion.2.refs_7_ = bf16[48,3584]{1,0:T(8,128)(2,1)} fusion(bf16[256,3584]{1,0:T(8,128)(2,1)} %together.17, s32[256]{0:T(256)} %copy-done.16, pred[256]{0:T(512)(128)(4,1)} %get-tuple-element.551), kind=kOutput, calls=%fused_computation.6 | convolution fusion | flops 88276992 | bytes 2180352 | tf_op jit(solution)/shard_map/dot_general | solution.py:39
  83.7 2.3 collective-permute-done.38.refs_0_
  86.0 3.2 %collective-permute-start.47 = (bf16[48,3584]{1,0:T(8,128)(2,1)}, bf16[48,3584]{1,0:T(8,128)(2,1)S(1)}, u32[]{:S(2)}, u32[]{:S(2)}) collective-permute-start(bf16[48,3584]{1,0:T(8,128)(2,1)} %get-tuple-element.512), channel_id=1, source_target_pairs={{0,2},{1,3},{2,0},{3,1},{4,6},{5,7},{6,4},{7,5},{8,10},{9,11},{10,... | collective-permute-start | bytes 1032200 | tf_op jit(solution)/shard_map/ppermute | solution.py:373
  94.7 10.4 %collective-permute-done.47 = bf16[48,3584]{1,0:T(8,128)(2,1)S(1)} collective-permute-done((bf16[48,3584]{1,0:T(8,128)(2,1)}, bf16[48,3584]{1,0:T(8,128)(2,1)S(1)}, u32[]{:S(2)}, u32[]{:S(2)}) %collective-permute-start.47) | collective-permute-done | bytes 344096 | tf_op jit(solution)/shard_map/ppermute | solution.py:373
  106.6 9.4 %collective-permute-done.48 = bf16[48,3584]{1,0:T(8,128)(2,1)S(1)} collective-permute-done((bf16[48,3584]{1,0:T(8,128)(2,1)}, bf16[48,3584]{1,0:T(8,128)(2,1)S(1)}, u32[]{:S(2)}, u32[]{:S(2)}) %collective-permute-start.48) | collective-permute-done | bytes 344096 | tf_op jit(solution)/shard_map/ppermute | solution.py:373
  121.5 7.2 %collective-permute-done.46.refs_3_ = bf16[144,3584]{1,0:T(8,128)(2,1)} collective-permute-done((bf16[144,3584]{1,0:T(8,128)(2,1)}, bf16[144,3584]{1,0:T(8,128)(2,1)}, u32[]{:S(2)}, u32[]{:S(2)}) %collective-permute-start.46) | collective-permute-done | bytes 1032224 | tf_op jit(solution)/shard_map/ppermute | solution.py:381
  131.3 12.3 %collective-permute-done.54.refs_0_ = bf16[144,3584]{1,0:T(8,128)(2,1)S(1)} collective-permute-done((bf16[144,3584]{1,0:T(8,128)(2,1)}, bf16[144,3584]{1,0:T(8,128)(2,1)S(1)}, u32[]{:S(2)}, u32[]{:S(2)}) %collective-permute-start.54) | collective-permute-done | bytes 1032224 | tf_op jit(solution)/shard_map/ppermute | solution.py:381
  152.3 26.8 %collective-permute-done.55.refs_0_ = bf16[192,3584]{1,0:T(8,128)(2,1)} collective-permute-done((bf16[192,3584]{1,0:T(8,128)(2,1)S(1)}, bf16[192,3584]{1,0:T(8,128)(2,1)}, u32[]{:S(2)}, u32[]{:S(2)}) %collective-permute-start.55) | collective-permute-done | bytes 1376288 | tf_op jit(solution)/shard_map/ppermute | solution.py:377
  179.1 52.3 %conditional.1 = (bf16[3584,256]{1,0:T(8,128)(2,1)}, bf16[3584,256]{1,0:T(8,128)(2,1)}, bf16[256,3584]{1,0:T(8,128)(2,1)}, bf16[3,448,256]{2,1,0:T(8,128)(2,1)S(1)}) conditional(s32[]{:T(128)} %clamp.3, (bf16[192,3584]{1,0:T(8,128)(2,1)}, bf16[3,448,256]{2,1,0:T(8,128)(2,1)}, bf16[192,3584]{1,0:T(8,128)(2,1)}, ...), branch_computations={%region_2.3_spmd, %region_3.4_spmd, %region_4.5_spmd, %region_5.6_... | conditional | flops 8456749056 | bytes 61243760 | solution.py:531
  182.8 15.1 %collective-permute-done.7.refs_0_ = bf16[192,3584]{1,0:T(8,128)(2,1)} collective-permute-done((bf16[192,3584]{1,0:T(8,128)(2,1)}, bf16[192,3584]{1,0:T(8,128)(2,1)}, u32[]{:S(2)}, u32[]{:S(2)}) %collective-permute-start.7) | collective-permute-done | bytes 1376288 | tf_op jit(solution)/shard_map/cond/branch_1_fun/ppermute | solution.py:381
  202.3 25.6 %cold_terms.5 = (bf16[3584,256]{1,0:T(8,128)(2,1)}, bf16[3584,256]{1,0:T(8,128)(2,1)}, bf16[256,3584]{1,0:T(8,128)(2,1)}, s32[8,128]{1,0:T(8,128)}) custom-call(s32[4]{0:T(128)S(1)} %get-tuple-element.337.refs_0_, bf16[96,3584]{1,0:T(8,128)(2,1)S(1)} %get-tuple-element.338.refs_1_, bf16[96,3584]{1,0:T(8,128)(2,1)} %get-tuple-element.339.refs_2_, ...), custom_call_target="tpu_custom_call" | custom-call | flops 8455716864 | bytes 22020096 | tf_op jit(solution)/shard_map/cond/branch_1_fun/cold_terms/pallas_call | solution.py:334
  229.8 1.7 add_select_fusion.1
  (147 shorter events, 55.7 us)
Async XLA Ops:
  14.9 26.9 %collective-permute-start.36 = (bf16[48,3584]{1,0:T(8,128)(2,1)}, bf16[48,3584]{1,0:T(8,128)(2,1)}, u32[]{:S(2)}, u32[]{:S(2)}) collective-permute-start(bf16[48,3584]{1,0:T(8,128)(2,1)} %convolution_convert_fusion.7), channel_id=1, source_target_pairs={{0,4},{1,5},{2,6},{3,7},{4,0},{5,1},{6,2},{7,3},{8,12},{9,13},{10,... | collective-permute-start | bytes 1032200 | tf_op jit(solution)/shard_map/ppermute | solution.py:373
  19.9 22.0 %collective-permute-start.37 = (bf16[48,3584]{1,0:T(8,128)(2,1)}, bf16[48,3584]{1,0:T(8,128)(2,1)S(1)}, u32[]{:S(2)}, u32[]{:S(2)}) collective-permute-start(bf16[48,3584]{1,0:T(8,128)(2,1)} %convolution_convert_fusion.6), channel_id=1, source_target_pairs={{0,6},{1,7},{2,4},{3,5},{4,2},{5,3},{6,0},{7,1},{8,14},{9,15},{10,... | collective-permute-start | bytes 1032200 | tf_op jit(solution)/shard_map/ppermute | solution.py:373
  21.5 21.5 %collective-permute-start.33 = (bf16[96,3584]{1,0:T(8,128)(2,1)S(1)}, bf16[96,3584]{1,0:T(8,128)(2,1)}, u32[]{:S(2)}, u32[]{:S(2)}) collective-permute-start(bf16[96,3584]{1,0:T(8,128)(2,1)S(1)} %together.15.refs_0_), channel_id=1, source_target_pairs={{0,8},{1,17},{2,10},{3,19},{4,12},{5,21},{6,14},{7,23},{8,0},{9,25... | collective-permute-start | bytes 2064392 | tf_op jit(solution)/shard_map/ppermute | solution.py:377
  23.3 19.8 %collective-permute-start.34 = (bf16[96,3584]{1,0:T(8,128)(2,1)S(1)}, bf16[96,3584]{1,0:T(8,128)(2,1)}, u32[]{:S(2)}, u32[]{:S(2)}) collective-permute-start(bf16[96,3584]{1,0:T(8,128)(2,1)S(1)} %together.15.refs_0_), channel_id=1, source_target_pairs={{0,16},{1,9},{2,18},{3,11},{4,20},{5,13},{6,22},{7,15},{8,24},{9,1... | collective-permute-start | bytes 2064392 | tf_op jit(solution)/shard_map/ppermute | solution.py:381
  43.1 21.0 %collective-permute-start.41 = (bf16[48,3584]{1,0:T(8,128)(2,1)}, bf16[48,3584]{1,0:T(8,128)(2,1)S(1)}, u32[]{:S(2)}, u32[]{:S(2)}) collective-permute-start(bf16[48,3584]{1,0:T(8,128)(2,1)} %get-tuple-element.507), channel_id=1, source_target_pairs={{0,2},{1,3},{2,0},{3,1},{4,6},{5,7},{6,4},{7,5},{8,10},{9,11},{10,... | collective-permute-start | bytes 1032200 | tf_op jit(solution)/shard_map/ppermute | solution.py:373
  50.1 26.9 %collective-permute-start.42 = (bf16[48,3584]{1,0:T(8,128)(2,1)}, bf16[48,3584]{1,0:T(8,128)(2,1)S(1)}, u32[]{:S(2)}, u32[]{:S(2)}) collective-permute-start(bf16[48,3584]{1,0:T(8,128)(2,1)} %get-tuple-element.508), channel_id=1, source_target_pairs={{0,4},{1,5},{2,6},{3,7},{4,0},{5,1},{6,2},{7,3},{8,12},{9,13},{10,... | collective-permute-start | bytes 1032200 | tf_op jit(solution)/shard_map/ppermute | solution.py:373
  51.2 25.8 %collective-permute-start.43 = (bf16[48,3584]{1,0:T(8,128)(2,1)}, bf16[48,3584]{1,0:T(8,128)(2,1)S(1)}, u32[]{:S(2)}, u32[]{:S(2)}) collective-permute-start(bf16[48,3584]{1,0:T(8,128)(2,1)} %get-tuple-element.509), channel_id=1, source_target_pairs={{0,6},{1,7},{2,4},{3,5},{4,2},{5,3},{6,0},{7,1},{8,14},{9,15},{10,... | collective-permute-start | bytes 1032200 | tf_op jit(solution)/shard_map/ppermute | solution.py:373
  55.1 30.9 %collective-permute-start.39 = (bf16[144,3584]{1,0:T(8,128)(2,1)S(1)}, bf16[144,3584]{1,0:T(8,128)(2,1)}, u32[]{:S(2)}, u32[]{:S(2)}) collective-permute-start(bf16[144,3584]{1,0:T(8,128)(2,1)S(1)} %get-tuple-element.506.refs_1_), channel_id=1, source_target_pairs={{0,8},{1,17},{2,10},{3,19},{4,12},{5,21},{6,14},{7,23},{8,0},{9,25... | collective-permute-start | bytes 3096584 | tf_op jit(solution)/shard_map/ppermute | solution.py:377
  56.6 29.4 %collective-permute-start.40 = (bf16[144,3584]{1,0:T(8,128)(2,1)S(1)}, bf16[144,3584]{1,0:T(8,128)(2,1)}, u32[]{:S(2)}, u32[]{:S(2)}) collective-permute-start(bf16[144,3584]{1,0:T(8,128)(2,1)S(1)} %get-tuple-element.506.refs_1_), channel_id=1, source_target_pairs={{0,16},{1,9},{2,18},{3,11},{4,20},{5,13},{6,22},{7,15},{8,24},{9,1... | collective-permute-start | bytes 3096584 | tf_op jit(solution)/shard_map/ppermute | solution.py:381
  64.1 21.9 %collective-permute-start.38 = (bf16[96,3584]{1,0:T(8,128)(2,1)}, bf16[96,3584]{1,0:T(8,128)(2,1)}, u32[]{:S(2)}, u32[]{:S(2)}) collective-permute-start(bf16[96,3584]{1,0:T(8,128)(2,1)} %get-tuple-element.505.refs_2_), channel_id=1, source_target_pairs={{0,16},{1,9},{2,18},{3,11},{4,20},{5,13},{6,22},{7,15},{8,24},{9,1... | collective-permute-start | bytes 2064392 | tf_op jit(solution)/shard_map/ppermute | solution.py:381
  86.0 19.1 %collective-permute-start.47 = (bf16[48,3584]{1,0:T(8,128)(2,1)}, bf16[48,3584]{1,0:T(8,128)(2,1)S(1)}, u32[]{:S(2)}, u32[]{:S(2)}) collective-permute-start(bf16[48,3584]{1,0:T(8,128)(2,1)} %get-tuple-element.512), channel_id=1, source_target_pairs={{0,2},{1,3},{2,0},{3,1},{4,6},{5,7},{6,4},{7,5},{8,10},{9,11},{10,... | collective-permute-start | bytes 1032200 | tf_op jit(solution)/shard_map/ppermute | solution.py:373
  89.2 26.8 %collective-permute-start.48 = (bf16[48,3584]{1,0:T(8,128)(2,1)}, bf16[48,3584]{1,0:T(8,128)(2,1)S(1)}, u32[]{:S(2)}, u32[]{:S(2)}) collective-permute-start(bf16[48,3584]{1,0:T(8,128)(2,1)} %get-tuple-element.513), channel_id=1, source_target_pairs={{0,4},{1,5},{2,6},{3,7},{4,0},{5,1},{6,2},{7,3},{8,12},{9,13},{10,... | collective-permute-start | bytes 1032200 | tf_op jit(solution)/shard_map/ppermute | solution.py:373
  90.3 25.7 %collective-permute-start.49 = (bf16[48,3584]{1,0:T(8,128)(2,1)}, bf16[48,3584]{1,0:T(8,128)(2,1)S(1)}, u32[]{:S(2)}, u32[]{:S(2)}) collective-permute-start(bf16[48,3584]{1,0:T(8,128)(2,1)} %get-tuple-element.514), channel_id=1, source_target_pairs={{0,6},{1,7},{2,4},{3,5},{4,2},{5,3},{6,0},{7,1},{8,14},{9,15},{10,... | collective-permute-start | bytes 1032200 | tf_op jit(solution)/shard_map/ppermute | solution.py:373
  91.7 27.7 %collective-permute-start.44 = (bf16[144,3584]{1,0:T(8,128)(2,1)}, bf16[144,3584]{1,0:T(8,128)(2,1)S(1)}, u32[]{:S(2)}, u32[]{:S(2)}) collective-permute-start(bf16[144,3584]{1,0:T(8,128)(2,1)} %get-tuple-element.510.refs_10_), channel_id=1, source_target_pairs={{0,16},{1,9},{2,18},{3,11},{4,20},{5,13},{6,22},{7,15},{8,24},{9,1... | collective-permute-start | bytes 3096584 | tf_op jit(solution)/shard_map/ppermute | solution.py:381
  93.2 26.1 %collective-permute-start.45 = (bf16[144,3584]{1,0:T(8,128)(2,1)}, bf16[144,3584]{1,0:T(8,128)(2,1)S(1)}, u32[]{:S(2)}, u32[]{:S(2)}) collective-permute-start(bf16[144,3584]{1,0:T(8,128)(2,1)} %get-tuple-element.511.refs_1_), channel_id=1, source_target_pairs={{0,8},{1,17},{2,10},{3,19},{4,12},{5,21},{6,14},{7,23},{8,0},{9,25... | collective-permute-start | bytes 3096584 | tf_op jit(solution)/shard_map/ppermute | solution.py:377
  105.1 23.6 %collective-permute-start.46 = (bf16[144,3584]{1,0:T(8,128)(2,1)}, bf16[144,3584]{1,0:T(8,128)(2,1)}, u32[]{:S(2)}, u32[]{:S(2)}) collective-permute-start(bf16[144,3584]{1,0:T(8,128)(2,1)} %get-tuple-element.511.refs_1_), channel_id=1, source_target_pairs={{0,16},{1,9},{2,18},{3,11},{4,20},{5,13},{6,22},{7,15},{8,24},{9,1... | collective-permute-start | bytes 3096584 | tf_op jit(solution)/shard_map/ppermute | solution.py:381
  130.8 18.8 %collective-permute-start.63 = (bf16[144,3584]{1,0:T(8,128)(2,1)}, bf16[144,3584]{1,0:T(8,128)(2,1)}, u32[]{:S(2)}, u32[]{:S(2)}) collective-permute-start(bf16[144,3584]{1,0:T(8,128)(2,1)} %get-tuple-element.518.refs_17_), channel_id=1, source_target_pairs={{0,1},{1,0},{2,3},{3,2},{4,5},{5,4},{6,7},{7,6},{8,9},{9,8},{10,11... | collective-permute-start | bytes 3096584 | tf_op jit(solution)/shard_map/ppermute | solution.py:370
  146.6 32.6 %collective-permute-start.55 = (bf16[192,3584]{1,0:T(8,128)(2,1)S(1)}, bf16[192,3584]{1,0:T(8,128)(2,1)}, u32[]{:S(2)}, u32[]{:S(2)}) collective-permute-start(bf16[192,3584]{1,0:T(8,128)(2,1)S(1)} %get-tuple-element.520), channel_id=1, source_target_pairs={{0,8},{1,17},{2,10},{3,19},{4,12},{5,21},{6,14},{7,23},{8,0},{9,25... | collective-permute-start | bytes 4128776 | tf_op jit(solution)/shard_map/ppermute | solution.py:377
  148.0 31.1 %collective-permute-start.56 = (bf16[192,3584]{1,0:T(8,128)(2,1)S(1)}, bf16[192,3584]{1,0:T(8,128)(2,1)}, u32[]{:S(2)}, u32[]{:S(2)}) collective-permute-start(bf16[192,3584]{1,0:T(8,128)(2,1)S(1)} %get-tuple-element.520), channel_id=1, source_target_pairs={{0,16},{1,9},{2,18},{3,11},{4,20},{5,13},{6,22},{7,15},{8,24},{9,1... | collective-permute-start | bytes 4128776 | tf_op jit(solution)/shard_map/ppermute | solution.py:381
  149.6 29.6 %collective-permute-start.57 = (bf16[192,3584]{1,0:T(8,128)(2,1)S(1)}, bf16[192,3584]{1,0:T(8,128)(2,1)}, u32[]{:S(2)}, u32[]{:S(2)}) collective-permute-start(bf16[192,3584]{1,0:T(8,128)(2,1)S(1)} %get-tuple-element.520), channel_id=1, source_target_pairs={{0,1},{1,0},{2,3},{3,2},{4,5},{5,4},{6,7},{7,6},{8,9},{9,8},{10,11... | collective-permute-start | bytes 4128776 | tf_op jit(solution)/shard_map/ppermute | solution.py:370
  179.2 18.7 %collective-permute-start.7 = (bf16[192,3584]{1,0:T(8,128)(2,1)}, bf16[192,3584]{1,0:T(8,128)(2,1)}, u32[]{:S(2)}, u32[]{:S(2)}) collective-permute-start(bf16[192,3584]{1,0:T(8,128)(2,1)} %get-tuple-element.363.refs_26_), channel_id=1, source_target_pairs={{0,16},{1,9},{2,18},{3,11},{4,20},{5,13},{6,22},{7,15},{8,24},{9,1... | collective-permute-start | bytes 4128776 | tf_op jit(solution)/shard_map/cond/branch_1_fun/ppermute | solution.py:381
  182.2 18.4 %collective-permute-start.10 = (bf16[192,3584]{1,0:T(8,128)(2,1)}, bf16[192,3584]{1,0:T(8,128)(2,1)}, u32[]{:S(2)}, u32[]{:S(2)}) collective-permute-start(bf16[192,3584]{1,0:T(8,128)(2,1)} %get-tuple-element.363.refs_26_), channel_id=1, source_target_pairs={{0,1},{1,0},{2,3},{3,2},{4,5},{5,4},{6,7},{7,6},{8,9},{9,8},{10,11... | collective-permute-start | bytes 4128776 | tf_op jit(solution)/shard_map/cond/branch_1_fun/ppermute | solution.py:370
  197.9 31.9 %collective-permute-start.12 = (bf16[3,448,256]{2,1,0:T(8,128)(2,1)}, bf16[3,448,256]{2,1,0:T(8,128)(2,1)}, u32[]{:S(2)}, u32[]{:S(2)}) collective-permute-start(bf16[3,448,256]{2,1,0:T(8,128)(2,1)} %get-tuple-element.376), channel_id=1, source_target_pairs={{2,0},{3,1},{10,8},{11,9},{18,16},{19,17},{26,24},{27,25}} | collective-permute-start | bytes 2064392 | tf_op jit(solution)/shard_map/cond/branch_1_fun/ppermute | solution.py:511
  199.1 30.6 %collective-permute-start.13 = (bf16[3,448,256]{2,1,0:T(8,128)(2,1)}, bf16[3,448,256]{2,1,0:T(8,128)(2,1)}, u32[]{:S(2)}, u32[]{:S(2)}) collective-permute-start(bf16[3,448,256]{2,1,0:T(8,128)(2,1)} %get-tuple-element.377), channel_id=1, source_target_pairs={{2,4},{3,5},{10,12},{11,13},{18,20},{19,21},{26,28},{27,29}} | collective-permute-start | bytes 2064392 | tf_op jit(solution)/shard_map/cond/branch_1_fun/ppermute | solution.py:511
  (41 other events, 331.1 us)
where the time goes:
time: 235 us; the launch traced here: 232 us
  waiting for transfers between devices  120 us (51%)
  starting transfers between devices  47.2 us (20%)
  Pallas kernels  27 us (11%)
  matrix products  16.3 us (7%)
  other arithmetic  11.7 us (5%)
  local copies, waits for them, and re-layouts  7.91 us (3%)
    ppermute x9, waiting for transfers between devices, along(): lax.ppermute(array, 'expert', [(j, j ^ 2 * step) for j in range(experts)])  51.1 us
    ppermute x8, waiting for transfers between devices, second_way(): return lax.ppermute(array, ('dp', 'expert'), pairs)  36.9 us
    pallas_call x2, Pallas kernels, expert_call(): pl.pallas_call(kernel, out_shape=out_shape, in_specs=[pl.BlockSpec(memory...  27 us
    ppermute x4, waiting for transfers between devices, first_way(): return lax.ppermute(array, ('dp', 'expert'), pairs)  26.8 us
    ppermute x9, starting transfers between devices, along(): lax.ppermute(array, 'expert', [(j, j ^ 2 * step) for j in range(experts)])  20.5 us
    dot_general x9, matrix products, route_rows(): jnp.dot(selector, values, preferred_element_type=jnp.float32)  16.3 us
    ppermute x8, starting transfers between devices, second_way(): return lax.ppermute(array, ('dp', 'expert'), pairs)  12.2 us
    unnamed x41, local copies, waits for them, and re-layouts  5.58 us
  transfers between devices with their start and end apart: 45, of which 17 were waited for; matrix products, arithmetic and copies ran while one was open for 13% of the time, Pallas kernels for 12%

commit v1 on v0

--- a/solution.py
+++ b/solution.py
@@ -210,15 +210,20 @@
             gate_up_t[pl.ds(hidden_width, hidden_width), span] = up_grad.T.astype(jnp.bfloat16)
 
         if kind == "cold":
+            half = rows // block_rows // 2
+            early = needed(half - 1)
             fetch(needed(0), len(sizes))
-            for copy in copies(0, 0, 0, len(sizes)):
-                copy.wait()
 
             def each(i, carry):
                 forward(pl.multiple_of(i * block_rows, block_rows))
                 return carry
 
-            lax.fori_loop(0, rows // block_rows, each, 0)
+            for copy in copies(0, 0, 0, early):
+                copy.wait()
+            lax.fori_loop(0, half, each, 0)
+            for copy in copies(0, 0, early, len(sizes)):
+                copy.wait()
+            lax.fori_loop(half, rows // block_rows, each, 0)
         else:
             arrived = 0
             for block in range(rows // block_rows):
@@ -300,7 +305,7 @@
     width, hidden_width = weights[0].shape
     rows = sum(entry[-1] for entry in plan[0])
     block_rows = divisor(rows, 384 if kind == "hot" else 128, 128)
-    block_columns = divisor(width, 512 if kind == "hot" else 256, 128)
+    block_columns = divisor(width, 512, 128)
     bf16 = jnp.bfloat16
     scratch = [
         pltpu.VMEM((rows, width), bf16),
@@ -410,8 +415,8 @@
         slot = place - offset + capacity * holder
         return ((slots == slot[None, :]) & taken[None, :]).astype(jnp.bfloat16)
 
-    def rows(*wanted, of=values):
-        return route_rows(jnp.concatenate([selector(*w) for w in wanted], axis=0), of)
+    def rows(*wanted):
+        return route_rows(jnp.concatenate([selector(*w) for w in wanted], axis=0), values)
 
     weights = (w_gate[0], w_up[0], w_down[0])
     is_owner = me == hot_expert
@@ -445,21 +450,21 @@
         return tuple(chosen)
 
     near_unit = rows(("first", 0), ("rest", 0))
-    sent = {k: [rows((k, s)) for s in range(1, chips)] for k in ("first", "rest")}
+    sent = {k: [rows((k, s)) for s in range(1, chips)] for k in ("first", "rest", "second")}
+    own_second = rows(("second", 0))
 
 
     (near_unit,) = together([near_unit], sibling_weights)
     near_1, side_1 = first_way(near_unit), second_way(near_unit)
     got = [along(block, s) for s, block in enumerate(sent["first"], 1)]
     first_unit = jnp.concatenate(got, axis=0)
-    near_unit, near_1, side_1, first_unit, *sent["rest"] = together(
-        [near_unit, near_1, side_1, first_unit, *sent["rest"]]
-    )
+    near_unit, near_1, side_1, first_unit, *held = together(
+        [near_unit, near_1, side_1, first_unit, *sent["rest"], *sent["second"]]
+    )
+    sent["rest"], sent["second"] = held[: chips - 1], held[chips - 1 :]
     far_1 = second_way(near_1)
     near_2, side_2 = first_way(first_unit), second_way(first_unit)
     got = [along(block, s) for s, block in enumerate(sent["rest"], 1)]
-    (values,) = together([values], got[:1])
-    own_second, *sent["second"] = [rows(("second", s), of=values) for s in range(chips)]
     swapped_1 = [swap(a) for a in (near_unit, side_1, near_1)]
     rest_unit = jnp.concatenate(got, axis=0)
     far_1, first_unit, near_2, side_2, rest_unit, *sent["second"] = together([

time: 235 us -> 232 us (0.987); the launches traced: 232 us -> 233 us
  waiting for transfers between devices: 120 us -> 129 us
  starting transfers between devices: 47.2 us -> 41 us
  other arithmetic: 11.7 us -> 6.01 us
  matrix products: 16.3 us -> 19.9 us
  Pallas kernels: 27 us -> 23.9 us
  local copies, waits for them, and re-layouts: 7.91 us -> 10.9 us
    ppermute x3, waiting for transfers between devices: 0.01 us -> 19.9 us  [send(): return lax.ppermute(blocks[z], 'expert', pairs)]
    ppermute x8, waiting for transfers between devices: 36.9 us -> 20.1 us  [second_way(): return lax.ppermute(array, ('dp', 'expert'), pairs)]
    ppermute x8, starting transfers between devices: 12.2 us -> 7.6 us  [second_way(): return lax.ppermute(array, ('dp', 'expert'), pairs)]
    dot_general x9, matrix products: 16.3 us -> 19.9 us  [route_rows(): jnp.dot(selector, values, preferred_element_type=jnp.float32)]
    ppermute x4, waiting for transfers between devices: 26.8 us -> 30.1 us  [first_way(): return lax.ppermute(array, ('dp', 'expert'), pairs)]
    ppermute x9, waiting for transfers between devices: 51.1 us -> 54.2 us  [along(): lax.ppermute(array, 'expert', [(j, j ^ 2 * step) for j in range(experts)])]
    pallas_call x2, Pallas kernels: 27 us -> 23.9 us  [expert_call(): pl.pallas_call(kernel, out_shape=out_shape, in_specs=[pl.BlockSpec(memory...]
    unnamed x41 -> x35, local copies, waits for them, and re-layouts: 5.58 us -> 8.68 us
  transfers between devices with their start and end apart: 45 -> 45, of which waited for: 17 -> 18; matrix products, arithmetic and copies ran while one was open for 13% -> 12% of each run, Pallas kernels for 12% -> 10%
where the time goes in v1:
time: 232 us; the launch traced here: 233 us
  waiting for transfers between devices  129 us (56%)
  starting transfers between devices  41 us (18%)
  Pallas kernels  23.9 us (10%)
  matrix products  19.9 us (9%)
  local copies, waits for them, and re-layouts  10.9 us (5%)
  other arithmetic  6.01 us (3%)
    ppermute x9, waiting for transfers between devices, along(): lax.ppermute(array, 'expert', [(j, j ^ 2 * step) for j in range(experts)])  54.2 us
    ppermute x4, waiting for transfers between devices, first_way(): return lax.ppermute(array, ('dp', 'expert'), pairs)  30.1 us
    pallas_call x2, Pallas kernels, expert_call(): pl.pallas_call(kernel, out_shape=out_shape, in_specs=[pl.BlockSpec(memory...  23.9 us
    ppermute x8, waiting for transfers between devices, second_way(): return lax.ppermute(array, ('dp', 'expert'), pairs)  20.1 us
    dot_general x9, matrix products, route_rows(): jnp.dot(selector, values, preferred_element_type=jnp.float32)  19.9 us
    ppermute x3, waiting for transfers between devices, send(): return lax.ppermute(blocks[z], 'expert', pairs)  19.9 us
    ppermute x9, starting transfers between devices, along(): lax.ppermute(array, 'expert', [(j, j ^ 2 * step) for j in range(experts)])  17.9 us
    unnamed x35, local copies, waits for them, and re-layouts  8.68 us
  transfers between devices with their start and end apart: 45, of which 18 were waited for; matrix products, arithmetic and copies ran while one was open for 12% of the time, Pallas kernels for 10%

profile of v1, /device:TPU:0, one launch (start us, length us, event | category | flops | bytes accessed | tf_op | source)
XLA Modules:
  0.0 233.0 jit_solution(588578723953233167)
XLA Ops:
  1.2 3.0 %broadcast_select_fusion.1 = (bf16[128,3584]{1,0:T(8,128)(2,1)S(1)}, bf16[128,3584]{1,0:T(8,128)(2,1)}) fusion(bf16[128,3584]{1,0:T(8,128)(2,1)} %param.12, pred[]{:T(512)S(6)} %eq.233, bf16[128,3584]{1,0:T(8,128)(2,1)} %param.13, f32[128]{0:T(128)} %param.14), kind=kLoop, calls=%fused_computation.19 | loop fusion | flops 2293760 | bytes 3670529 | tf_op jit(solution)/shard_map/jit(_where)/select_n | solution.py:389
  10.7 2.3 %convolution_convert_fusion.8 = bf16[48,3584]{1,0:T(8,128)(2,1)} fusion(s32[256]{0:T(256)S(1)} %get-tuple-element.565, pred[256]{0:T(512)(128)(4,1)S(1)} %get-tuple-element.562, bf16[128,3584]{1,0:T(8,128)(2,1)} %collective-permute-done.29, bf16[128,3584]{1,0:T(8,128)(2,1)S(1)} %get-tuple-element.555), kind=kOutput, calls=%fused_computation.12 | convolution fusion | flops 91947008 | bytes 2180352 | tf_op jit(solution)/shard_map/dot_general | solution.py:39
  13.0 2.7 %collective-permute-start.35 = (bf16[48,3584]{1,0:T(8,128)(2,1)}, bf16[48,3584]{1,0:T(8,128)(2,1)S(1)}, u32[]{:S(2)}, u32[]{:S(2)}) collective-permute-start(bf16[48,3584]{1,0:T(8,128)(2,1)} %convolution_convert_fusion.8), channel_id=1, source_target_pairs={{0,2},{1,3},{2,0},{3,1},{4,6},{5,7},{6,4},{7,5},{8,10},{9,11},{10,... | collective-permute-start | bytes 1032200 | tf_op jit(solution)/shard_map/ppermute | solution.py:378
  15.7 2.3 convolution_convert_fusion.7
  18.1 2.6 %collective-permute-start.36 = (bf16[48,3584]{1,0:T(8,128)(2,1)}, bf16[48,3584]{1,0:T(8,128)(2,1)S(1)}, u32[]{:S(2)}, u32[]{:S(2)}) collective-permute-start(bf16[48,3584]{1,0:T(8,128)(2,1)} %convolution_convert_fusion.7), channel_id=1, source_target_pairs={{0,4},{1,5},{2,6},{3,7},{4,0},{5,1},{6,2},{7,3},{8,12},{9,13},{10,... | collective-permute-start | bytes 1032200 | tf_op jit(solution)/shard_map/ppermute | solution.py:378
  20.6 2.3 convolution_convert_fusion.6
  23.0 2.3 %convolution_convert_fusion.2.refs_9_ = bf16[48,3584]{1,0:T(8,128)(2,1)} fusion(s32[256]{0:T(256)S(1)} %get-tuple-element.565, pred[256]{0:T(512)(128)(4,1)S(1)} %get-tuple-element.557, bf16[128,3584]{1,0:T(8,128)(2,1)} %collective-permute-done.29, bf16[128,3584]{1,0:T(8,128)(2,1)S(1)} %get-tuple-element.555), kind=kOutput, calls=%fused_computation.6 | convolution fusion | flops 91947008 | bytes 2180352 | tf_op jit(solution)/shard_map/dot_general | solution.py:39
  25.3 2.4 %convolution_convert_fusion.3.refs_8_ = bf16[48,3584]{1,0:T(8,128)(2,1)} fusion(s32[256]{0:T(256)S(1)} %get-tuple-element.565, pred[256]{0:T(512)(128)(4,1)S(1)} %get-tuple-element.558, bf16[128,3584]{1,0:T(8,128)(2,1)} %collective-permute-done.29, bf16[128,3584]{1,0:T(8,128)(2,1)S(1)} %get-tuple-element.555), kind=kOutput, calls=%fused_computation.7 | convolution fusion | flops 91947008 | bytes 2180352 | tf_op jit(solution)/shard_map/dot_general | solution.py:39
  27.7 2.5 %convolution_convert_fusion.refs_0_ = bf16[96,3584]{1,0:T(8,128)(2,1)} fusion(pred[48,256]{1,0:T(8,128)(4,1)S(1)} %get-tuple-element.568, pred[48,256]{1,0:T(8,128)(4,1)S(1)} %get-tuple-element.567, bf16[128,3584]{1,0:T(8,128)(2,1)} %collective-permute-done.29, bf16[128,3584]{1,0:T(8,128)(2,1)S(1)} %get-tuple-element.555), kind=kOutput, calls=%fused_computation.4 | convolution fusion | flops 180199424 | bytes 2547712 | tf_op jit(solution)/shard_map/dot_general | solution.py:39
  33.5 2.3 %convolution_convert_fusion.4.refs_7_ = bf16[48,3584]{1,0:T(8,128)(2,1)} fusion(s32[256]{0:T(256)S(1)} %get-tuple-element.565, pred[256]{0:T(512)(128)(4,1)S(1)} %get-tuple-element.559, bf16[128,3584]{1,0:T(8,128)(2,1)} %collective-permute-done.29, bf16[128,3584]{1,0:T(8,128)(2,1)S(1)} %get-tuple-element.555), kind=kOutput, calls=%fused_computation.8 | convolution fusion | flops 91947008 | bytes 2180352 | tf_op jit(solution)/shard_map/dot_general | solution.py:39
  35.8 9.1 %collective-permute-done.36 = bf16[48,3584]{1,0:T(8,128)(2,1)S(1)} collective-permute-done((bf16[48,3584]{1,0:T(8,128)(2,1)}, bf16[48,3584]{1,0:T(8,128)(2,1)S(1)}, u32[]{:S(2)}, u32[]{:S(2)}) %collective-permute-start.36) | collective-permute-done | bytes 344096 | tf_op jit(solution)/shard_map/ppermute | solution.py:378
  45.0 3.8 %collective-permute-done.33.refs_1_ = bf16[96,3584]{1,0:T(8,128)(2,1)} collective-permute-done((bf16[96,3584]{1,0:T(8,128)(2,1)}, bf16[96,3584]{1,0:T(8,128)(2,1)}, u32[]{:S(2)}, u32[]{:S(2)}) %collective-permute-start.33) | collective-permute-done | bytes 688160 | tf_op jit(solution)/shard_map/ppermute | solution.py:382
  48.8 3.3 %collective-permute-start.41 = (bf16[48,3584]{1,0:T(8,128)(2,1)}, bf16[48,3584]{1,0:T(8,128)(2,1)S(1)}, u32[]{:S(2)}, u32[]{:S(2)}) collective-permute-start(bf16[48,3584]{1,0:T(8,128)(2,1)} %get-tuple-element.510), channel_id=1, source_target_pairs={{0,2},{1,3},{2,0},{3,1},{4,6},{5,7},{6,4},{7,5},{8,10},{9,11},{10,... | collective-permute-start | bytes 1032200 | tf_op jit(solution)/shard_map/ppermute | solution.py:378
  57.6 7.0 %collective-permute-done.41 = bf16[48,3584]{1,0:T(8,128)(2,1)S(1)} collective-permute-done((bf16[48,3584]{1,0:T(8,128)(2,1)}, bf16[48,3584]{1,0:T(8,128)(2,1)S(1)}, u32[]{:S(2)}, u32[]{:S(2)}) %collective-permute-start.41) | collective-permute-done | bytes 344096 | tf_op jit(solution)/shard_map/ppermute | solution.py:378
  66.6 15.4 %collective-permute-done.42 = bf16[48,3584]{1,0:T(8,128)(2,1)S(1)} collective-permute-done((bf16[48,3584]{1,0:T(8,128)(2,1)}, bf16[48,3584]{1,0:T(8,128)(2,1)S(1)}, u32[]{:S(2)}, u32[]{:S(2)}) %collective-permute-start.42) | collective-permute-done | bytes 344096 | tf_op jit(solution)/shard_map/ppermute | solution.py:378
  84.0 4.3 %collective-permute-start.47 = (bf16[48,3584]{1,0:T(8,128)(2,1)}, bf16[48,3584]{1,0:T(8,128)(2,1)S(1)}, u32[]{:S(2)}, u32[]{:S(2)}) collective-permute-start(bf16[48,3584]{1,0:T(8,128)(2,1)} %get-tuple-element.518), channel_id=1, source_target_pairs={{0,2},{1,3},{2,0},{3,1},{4,6},{5,7},{6,4},{7,5},{8,10},{9,11},{10,... | collective-permute-start | bytes 1032200 | tf_op jit(solution)/shard_map/ppermute | solution.py:378
  91.8 12.4 %collective-permute-done.47 = bf16[48,3584]{1,0:T(8,128)(2,1)S(1)} collective-permute-done((bf16[48,3584]{1,0:T(8,128)(2,1)}, bf16[48,3584]{1,0:T(8,128)(2,1)S(1)}, u32[]{:S(2)}, u32[]{:S(2)}) %collective-permute-start.47) | collective-permute-done | bytes 344096 | tf_op jit(solution)/shard_map/ppermute | solution.py:378
  104.7 10.4 %collective-permute-done.48 = bf16[48,3584]{1,0:T(8,128)(2,1)S(1)} collective-permute-done((bf16[48,3584]{1,0:T(8,128)(2,1)}, bf16[48,3584]{1,0:T(8,128)(2,1)S(1)}, u32[]{:S(2)}, u32[]{:S(2)}) %collective-permute-start.48) | collective-permute-done | bytes 344096 | tf_op jit(solution)/shard_map/ppermute | solution.py:378
  120.6 6.2 %collective-permute-done.46.refs_3_ = bf16[144,3584]{1,0:T(8,128)(2,1)} collective-permute-done((bf16[144,3584]{1,0:T(8,128)(2,1)S(1)}, bf16[144,3584]{1,0:T(8,128)(2,1)}, u32[]{:S(2)}, u32[]{:S(2)}) %collective-permute-start.46) | collective-permute-done | bytes 1032224 | tf_op jit(solution)/shard_map/ppermute | solution.py:386
  128.4 13.3 %collective-permute-done.54.refs_0_ = bf16[144,3584]{1,0:T(8,128)(2,1)S(1)} collective-permute-done((bf16[144,3584]{1,0:T(8,128)(2,1)}, bf16[144,3584]{1,0:T(8,128)(2,1)S(1)}, u32[]{:S(2)}, u32[]{:S(2)}) %collective-permute-start.54) | collective-permute-done | bytes 1032224 | tf_op jit(solution)/shard_map/ppermute | solution.py:386
  150.5 26.2 %collective-permute-done.55.refs_0_ = bf16[192,3584]{1,0:T(8,128)(2,1)S(1)} collective-permute-done((bf16[192,3584]{1,0:T(8,128)(2,1)S(1)}, bf16[192,3584]{1,0:T(8,128)(2,1)S(1)}, u32[]{:S(2)}, u32[]{:S(2)}) %collective-permute-start.55) | collective-permute-done | bytes 1376288 | tf_op jit(solution)/shard_map/ppermute | solution.py:382
  178.9 53.2 %conditional.1 = (bf16[3584,256]{1,0:T(8,128)(2,1)}, bf16[3584,256]{1,0:T(8,128)(2,1)}, bf16[256,3584]{1,0:T(8,128)(2,1)}, bf16[3,448,256]{2,1,0:T(8,128)(2,1)S(1)}) conditional(s32[]{:T(128)} %clamp.3, (bf16[192,3584]{1,0:T(8,128)(2,1)}, bf16[3,448,256]{2,1,0:T(8,128)(2,1)}, bf16[192,3584]{1,0:T(8,128)(2,1)}, ...), branch_computations={%region_2.3_spmd, %region_3.4_spmd, %region_4.5_spmd, %region_5.6_... | conditional | flops 8456749056 | bytes 61243760 | solution.py:536
  181.6 19.9 %collective-permute-done.22.refs_1_ = bf16[3,448,256]{2,1,0:T(8,128)(2,1)} collective-permute-done((bf16[3,448,256]{2,1,0:T(8,128)(2,1)}, bf16[3,448,256]{2,1,0:T(8,128)(2,1)}, u32[]{:S(2)}, u32[]{:S(2)}) %collective-permute-start.22) | collective-permute-done | bytes 688160 | tf_op jit(solution)/shard_map/cond/branch_3_fun/ppermute | solution.py:516
  205.9 22.5 %cold_terms.7 = (bf16[3584,256]{1,0:T(8,128)(2,1)}, bf16[3584,256]{1,0:T(8,128)(2,1)}, bf16[256,3584]{1,0:T(8,128)(2,1)}, s32[8,128]{1,0:T(8,128)}) custom-call(s32[4]{0:T(128)S(1)} %get-tuple-element.419.refs_0_, bf16[96,3584]{1,0:T(8,128)(2,1)} %get-tuple-element.420.refs_1_, bf16[96,3584]{1,0:T(8,128)(2,1)} %get-tuple-element.421.refs_2_, ...), custom_call_target="tpu_custom_call" | custom-call | flops 8455716864 | bytes 22020096 | tf_op jit(solution)/shard_map/cond/branch_3_fun/cold_terms/pallas_call | solution.py:339
  (139 shorter events, 52.2 us)
Async XLA Ops:
  4.2 23.5 %collective-permute-start.30 = (bf16[3584,256]{1,0:T(8,128)(2,1)S(1)}, bf16[3584,256]{1,0:T(8,128)(2,1)}, u32[]{:S(2)}, u32[]{:S(2)}) collective-permute-start(bf16[3584,256]{1,0:T(8,128)(2,1)S(1)} %bitcast.24), channel_id=1, source_target_pairs={{0,1},{1,0},{2,3},{3,2},{4,5},{5,4},{6,7},{7,6},{8,9},{9,8},{10,11... | collective-permute-start | bytes 5505032 | tf_op jit(solution)/shard_map/ppermute | solution.py:375
  4.7 25.5 %collective-permute-start.31 = (bf16[3584,256]{1,0:T(8,128)(2,1)}, bf16[3584,256]{1,0:T(8,128)(2,1)}, u32[]{:S(2)}, u32[]{:S(2)}) collective-permute-start(bf16[3584,256]{1,0:T(8,128)(2,1)} %bitcast.6.refs_26_), channel_id=1, source_target_pairs={{0,1},{1,0},{2,3},{3,2},{4,5},{5,4},{6,7},{7,6},{8,9},{9,8},{10,11... | collective-permute-start | bytes 5505032 | tf_op jit(solution)/shard_map/ppermute | solution.py:375
  4.8 25.4 %collective-permute-start.32 = (bf16[256,3584]{1,0:T(8,128)(2,1)}, bf16[256,3584]{1,0:T(8,128)(2,1)}, u32[]{:S(2)}, u32[]{:S(2)}) collective-permute-start(bf16[256,3584]{1,0:T(8,128)(2,1)} %bitcast.7.refs_27_), channel_id=1, source_target_pairs={{0,1},{1,0},{2,3},{3,2},{4,5},{5,4},{6,7},{7,6},{8,9},{9,8},{10,11... | collective-permute-start | bytes 5505032 | tf_op jit(solution)/shard_map/ppermute | solution.py:375
  13.0 22.8 %collective-permute-start.35 = (bf16[48,3584]{1,0:T(8,128)(2,1)}, bf16[48,3584]{1,0:T(8,128)(2,1)S(1)}, u32[]{:S(2)}, u32[]{:S(2)}) collective-permute-start(bf16[48,3584]{1,0:T(8,128)(2,1)} %convolution_convert_fusion.8), channel_id=1, source_target_pairs={{0,2},{1,3},{2,0},{3,1},{4,6},{5,7},{6,4},{7,5},{8,10},{9,11},{10,... | collective-permute-start | bytes 1032200 | tf_op jit(solution)/shard_map/ppermute | solution.py:378
  18.1 26.8 %collective-permute-start.36 = (bf16[48,3584]{1,0:T(8,128)(2,1)}, bf16[48,3584]{1,0:T(8,128)(2,1)S(1)}, u32[]{:S(2)}, u32[]{:S(2)}) collective-permute-start(bf16[48,3584]{1,0:T(8,128)(2,1)} %convolution_convert_fusion.7), channel_id=1, source_target_pairs={{0,4},{1,5},{2,6},{3,7},{4,0},{5,1},{6,2},{7,3},{8,12},{9,13},{10,... | collective-permute-start | bytes 1032200 | tf_op jit(solution)/shard_map/ppermute | solution.py:378
  52.1 31.0 %collective-permute-start.39 = (bf16[144,3584]{1,0:T(8,128)(2,1)S(1)}, bf16[144,3584]{1,0:T(8,128)(2,1)}, u32[]{:S(2)}, u32[]{:S(2)}) collective-permute-start(bf16[144,3584]{1,0:T(8,128)(2,1)S(1)} %get-tuple-element.509.refs_1_), channel_id=1, source_target_pairs={{0,8},{1,17},{2,10},{3,19},{4,12},{5,21},{6,14},{7,23},{8,0},{9,25... | collective-permute-start | bytes 3096584 | tf_op jit(solution)/shard_map/ppermute | solution.py:382
  53.6 29.6 %collective-permute-start.40 = (bf16[144,3584]{1,0:T(8,128)(2,1)S(1)}, bf16[144,3584]{1,0:T(8,128)(2,1)S(1)}, u32[]{:S(2)}, u32[]{:S(2)}) collective-permute-start(bf16[144,3584]{1,0:T(8,128)(2,1)S(1)} %get-tuple-element.509.refs_1_), channel_id=1, source_target_pairs={{0,16},{1,9},{2,18},{3,11},{4,20},{5,13},{6,22},{7,15},{8,24},{9,1... | collective-permute-start | bytes 3096584 | tf_op jit(solution)/shard_map/ppermute | solution.py:386
  55.1 26.9 %collective-permute-start.42 = (bf16[48,3584]{1,0:T(8,128)(2,1)}, bf16[48,3584]{1,0:T(8,128)(2,1)S(1)}, u32[]{:S(2)}, u32[]{:S(2)}) collective-permute-start(bf16[48,3584]{1,0:T(8,128)(2,1)} %get-tuple-element.511), channel_id=1, source_target_pairs={{0,4},{1,5},{2,6},{3,7},{4,0},{5,1},{6,2},{7,3},{8,12},{9,13},{10,... | collective-permute-start | bytes 1032200 | tf_op jit(solution)/shard_map/ppermute | solution.py:378
  56.2 25.8 %collective-permute-start.43 = (bf16[48,3584]{1,0:T(8,128)(2,1)}, bf16[48,3584]{1,0:T(8,128)(2,1)S(1)}, u32[]{:S(2)}, u32[]{:S(2)}) collective-permute-start(bf16[48,3584]{1,0:T(8,128)(2,1)} %get-tuple-element.512), channel_id=1, source_target_pairs={{0,6},{1,7},{2,4},{3,5},{4,2},{5,3},{6,0},{7,1},{8,14},{9,15},{10,... | collective-permute-start | bytes 1032200 | tf_op jit(solution)/shard_map/ppermute | solution.py:378
  84.0 20.2 %collective-permute-start.47 = (bf16[48,3584]{1,0:T(8,128)(2,1)}, bf16[48,3584]{1,0:T(8,128)(2,1)S(1)}, u32[]{:S(2)}, u32[]{:S(2)}) collective-permute-start(bf16[48,3584]{1,0:T(8,128)(2,1)} %get-tuple-element.518), channel_id=1, source_target_pairs={{0,2},{1,3},{2,0},{3,1},{4,6},{5,7},{6,4},{7,5},{8,10},{9,11},{10,... | collective-permute-start | bytes 1032200 | tf_op jit(solution)/shard_map/ppermute | solution.py:378
  88.3 26.8 %collective-permute-start.48 = (bf16[48,3584]{1,0:T(8,128)(2,1)}, bf16[48,3584]{1,0:T(8,128)(2,1)S(1)}, u32[]{:S(2)}, u32[]{:S(2)}) collective-permute-start(bf16[48,3584]{1,0:T(8,128)(2,1)} %get-tuple-element.519), channel_id=1, source_target_pairs={{0,4},{1,5},{2,6},{3,7},{4,0},{5,1},{6,2},{7,3},{8,12},{9,13},{10,... | collective-permute-start | bytes 1032200 | tf_op jit(solution)/shard_map/ppermute | solution.py:378
  89.3 25.8 %collective-permute-start.49 = (bf16[48,3584]{1,0:T(8,128)(2,1)}, bf16[48,3584]{1,0:T(8,128)(2,1)S(1)}, u32[]{:S(2)}, u32[]{:S(2)}) collective-permute-start(bf16[48,3584]{1,0:T(8,128)(2,1)} %get-tuple-element.520), channel_id=1, source_target_pairs={{0,6},{1,7},{2,4},{3,5},{4,2},{5,3},{6,0},{7,1},{8,14},{9,15},{10,... | collective-permute-start | bytes 1032200 | tf_op jit(solution)/shard_map/ppermute | solution.py:378
  90.8 27.7 %collective-permute-start.44 = (bf16[144,3584]{1,0:T(8,128)(2,1)}, bf16[144,3584]{1,0:T(8,128)(2,1)S(1)}, u32[]{:S(2)}, u32[]{:S(2)}) collective-permute-start(bf16[144,3584]{1,0:T(8,128)(2,1)} %get-tuple-element.516.refs_10_), channel_id=1, source_target_pairs={{0,16},{1,9},{2,18},{3,11},{4,20},{5,13},{6,22},{7,15},{8,24},{9,1... | collective-permute-start | bytes 3096584 | tf_op jit(solution)/shard_map/ppermute | solution.py:386
  91.3 27.2 %collective-permute-start.45 = (bf16[144,3584]{1,0:T(8,128)(2,1)S(1)}, bf16[144,3584]{1,0:T(8,128)(2,1)S(1)}, u32[]{:S(2)}, u32[]{:S(2)}) collective-permute-start(bf16[144,3584]{1,0:T(8,128)(2,1)S(1)} %get-tuple-element.517.refs_1_), channel_id=1, source_target_pairs={{0,8},{1,17},{2,10},{3,19},{4,12},{5,21},{6,14},{7,23},{8,0},{9,25... | collective-permute-start | bytes 3096584 | tf_op jit(solution)/shard_map/ppermute | solution.py:382
  104.2 22.7 %collective-permute-start.46 = (bf16[144,3584]{1,0:T(8,128)(2,1)S(1)}, bf16[144,3584]{1,0:T(8,128)(2,1)}, u32[]{:S(2)}, u32[]{:S(2)}) collective-permute-start(bf16[144,3584]{1,0:T(8,128)(2,1)S(1)} %get-tuple-element.517.refs_1_), channel_id=1, source_target_pairs={{0,16},{1,9},{2,18},{3,11},{4,20},{5,13},{6,22},{7,15},{8,24},{9,1... | collective-permute-start | bytes 3096584 | tf_op jit(solution)/shard_map/ppermute | solution.py:386
  144.5 32.2 %collective-permute-start.55 = (bf16[192,3584]{1,0:T(8,128)(2,1)S(1)}, bf16[192,3584]{1,0:T(8,128)(2,1)S(1)}, u32[]{:S(2)}, u32[]{:S(2)}) collective-permute-start(bf16[192,3584]{1,0:T(8,128)(2,1)S(1)} %get-tuple-element.526), channel_id=1, source_target_pairs={{0,8},{1,17},{2,10},{3,19},{4,12},{5,21},{6,14},{7,23},{8,0},{9,25... | collective-permute-start | bytes 4128776 | tf_op jit(solution)/shard_map/ppermute | solution.py:382
  146.1 30.5 %collective-permute-start.56 = (bf16[192,3584]{1,0:T(8,128)(2,1)S(1)}, bf16[192,3584]{1,0:T(8,128)(2,1)S(1)}, u32[]{:S(2)}, u32[]{:S(2)}) collective-permute-start(bf16[192,3584]{1,0:T(8,128)(2,1)S(1)} %get-tuple-element.526), channel_id=1, source_target_pairs={{0,16},{1,9},{2,18},{3,11},{4,20},{5,13},{6,22},{7,15},{8,24},{9,1... | collective-permute-start | bytes 4128776 | tf_op jit(solution)/shard_map/ppermute | solution.py:386
  146.7 30.0 %collective-permute-start.57 = (bf16[192,3584]{1,0:T(8,128)(2,1)S(1)}, bf16[192,3584]{1,0:T(8,128)(2,1)S(1)}, u32[]{:S(2)}, u32[]{:S(2)}) collective-permute-start(bf16[192,3584]{1,0:T(8,128)(2,1)S(1)} %get-tuple-element.526), channel_id=1, source_target_pairs={{0,1},{1,0},{2,3},{3,2},{4,5},{5,4},{6,7},{7,6},{8,9},{9,8},{10,11... | collective-permute-start | bytes 4128776 | tf_op jit(solution)/shard_map/ppermute | solution.py:375
  178.9 22.6 %collective-permute-start.21 = (bf16[192,3584]{1,0:T(8,128)(2,1)}, bf16[192,3584]{1,0:T(8,128)(2,1)}, u32[]{:S(2)}, u32[]{:S(2)}) collective-permute-start(bf16[192,3584]{1,0:T(8,128)(2,1)} %get-tuple-element.445.refs_26_), channel_id=1, source_target_pairs={{0,16},{1,9},{2,18},{3,11},{4,20},{5,13},{6,22},{7,15},{8,24},{9,1... | collective-permute-start | bytes 4128776 | tf_op jit(solution)/shard_map/cond/branch_3_fun/ppermute | solution.py:386
  179.4 22.1 %collective-permute-start.22 = (bf16[3,448,256]{2,1,0:T(8,128)(2,1)}, bf16[3,448,256]{2,1,0:T(8,128)(2,1)}, u32[]{:S(2)}, u32[]{:S(2)}) collective-permute-start(bf16[3,448,256]{2,1,0:T(8,128)(2,1)} %get-tuple-element.447), channel_id=1, source_target_pairs={{6,0},{7,1},{14,8},{15,9},{22,16},{23,17},{30,24},{31,25}} | collective-permute-start | bytes 2064392 | tf_op jit(solution)/shard_map/cond/branch_3_fun/ppermute | solution.py:516
  180.7 23.9 %collective-permute-start.24 = (bf16[192,3584]{1,0:T(8,128)(2,1)}, bf16[192,3584]{1,0:T(8,128)(2,1)}, u32[]{:S(2)}, u32[]{:S(2)}) collective-permute-start(bf16[192,3584]{1,0:T(8,128)(2,1)} %get-tuple-element.445.refs_26_), channel_id=1, source_target_pairs={{0,1},{1,0},{2,3},{3,2},{4,5},{5,4},{6,7},{7,6},{8,9},{9,8},{10,11... | collective-permute-start | bytes 4128776 | tf_op jit(solution)/shard_map/cond/branch_3_fun/ppermute | solution.py:375
  181.5 23.1 %collective-permute-start.23 = (bf16[192,3584]{1,0:T(8,128)(2,1)}, bf16[192,3584]{1,0:T(8,128)(2,1)}, u32[]{:S(2)}, u32[]{:S(2)}) collective-permute-start(bf16[192,3584]{1,0:T(8,128)(2,1)} %get-tuple-element.446.refs_27_), channel_id=1, source_target_pairs={{0,1},{1,0},{2,3},{3,2},{4,5},{5,4},{6,7},{7,6},{8,9},{9,8},{10,11... | collective-permute-start | bytes 4128776 | tf_op jit(solution)/shard_map/cond/branch_3_fun/ppermute | solution.py:375
  201.5 28.7 %collective-permute-start.26 = (bf16[3,448,256]{2,1,0:T(8,128)(2,1)}, bf16[3,448,256]{2,1,0:T(8,128)(2,1)}, u32[]{:S(2)}, u32[]{:S(2)}) collective-permute-start(bf16[3,448,256]{2,1,0:T(8,128)(2,1)} %get-tuple-element.458), channel_id=1, source_target_pairs={{6,2},{7,3},{14,10},{15,11},{22,18},{23,19},{30,26},{31,27}} | collective-permute-start | bytes 2064392 | tf_op jit(solution)/shard_map/cond/branch_3_fun/ppermute | solution.py:516
  203.0 27.1 %collective-permute-start.27 = (bf16[3,448,256]{2,1,0:T(8,128)(2,1)}, bf16[3,448,256]{2,1,0:T(8,128)(2,1)}, u32[]{:S(2)}, u32[]{:S(2)}) collective-permute-start(bf16[3,448,256]{2,1,0:T(8,128)(2,1)} %get-tuple-element.459), channel_id=1, source_target_pairs={{6,4},{7,5},{14,12},{15,13},{22,20},{23,21},{30,28},{31,29}} | collective-permute-start | bytes 2064392 | tf_op jit(solution)/shard_map/cond/branch_3_fun/ppermute | solution.py:516
  (38 other events, 307.1 us)
